TPU v7x, 256 devices: a whole 4x4x8 slice. The times are simulated.
256 devices in a mesh: tm: 64 (over x, z, core), chan: 4 (over y).
Axes of the slice: x: 4, y: 4, z: 8, core: 2. Of those that a mesh axis runs over, the one named last changes fastest.
Arguments:
- features: bfloat16 [393216, 512], P('tm', 'chan'), may hold values from -6 to 6
- snake_alpha: float32 [512], P('chan'), may hold values from 0.5 to 3
- down_weight: bfloat16 [512, 16, 1024], P(None, None, 'chan'), may hold values from -0.0625 to 0.0625
- grad_out: bfloat16 [49152, 1024], P('tm', 'chan'), may hold values from -6 to 6
Outputs:
- encoded: bfloat16 [49152, 1024], P('tm', 'chan')
- grad_features: bfloat16 [393216, 512], P('tm', 'chan')
- grad_down: bfloat16 [1024, 16, 512], P('tm', None, 'chan')
All inputs are finite; a program needn't handle non-finite values.
Results may differ from a plain program's by a relative error of at most 0.0049.
Values may be sent and summed in bfloat16 or wider, within the bound.
No kernel may reach another device: no remote copies, remote signals or barrier semaphores. Data moves between devices by JAX's collectives and lax.ppermute only.
A program may use at most 128 MiB of HBM per device.

v0:
```python
import math
import jax
import jax.numpy as jnp
from jax import lax
from jax.sharding import PartitionSpec as P

STRIDE = 8


def with_halo(block, sides, width):
    for axis, dim in sides:
        count = lax.axis_size(axis)
        forward = [(i, i + 1) for i in range(count - 1)]
        backward = [(target, source) for source, target in forward]
        low = lax.ppermute(
            lax.slice_in_dim(block, block.shape[dim] - width, None, axis=dim), axis, forward
        )
        high = lax.ppermute(lax.slice_in_dim(block, 0, width, axis=dim), axis, backward)
        block = jnp.concatenate([low, block, high], axis=dim)
    return block


def snake(values, alpha):
    return values + jnp.sin(alpha * values) ** 2 / alpha


def shards(features, snake_alpha, down_weight, grad_out):
    frames = features.shape[0]
    local_chans = features.shape[1]
    blocks_out = frames // STRIDE
    offset = STRIDE // 2
    wide = features.astype(jnp.float32)
    snaked = snake(wide, snake_alpha).astype(jnp.bfloat16)
    padded = with_halo(snaked, (("tm", 0),), offset)
    local_tiled = padded.reshape(blocks_out + 1, STRIDE, local_chans)
    full_cols = lax.all_gather(padded, "chan", axis=1, tiled=True)
    tiled = full_cols.reshape(blocks_out + 1, STRIDE, full_cols.shape[1])
    encoded = (
        jnp.einsum(
            "ujr,rjp->up", tiled[:-1], down_weight[:, :STRIDE], preferred_element_type=jnp.float32
        )
        + jnp.einsum(
            "ujr,rjp->up", tiled[1:], down_weight[:, STRIDE:], preferred_element_type=jnp.float32
        )
    ).astype(jnp.bfloat16)
    grad_pad = with_halo(grad_out, (("tm", 0),), 1)
    grad_full = lax.all_gather(grad_pad, "chan", axis=1, tiled=True)
    spread = jnp.einsum(
        "up,rjp->ujr", grad_pad[1:], down_weight[:, :STRIDE], preferred_element_type=jnp.float32
    ) + jnp.einsum(
        "up,rjp->ujr", grad_pad[:-1], down_weight[:, STRIDE:], preferred_element_type=jnp.float32
    )
    partial_terms = spread.reshape(frames + STRIDE, down_weight.shape[0])[offset : offset + frames]
    grad_snaked = lax.psum_scatter(partial_terms, "chan", scatter_dimension=1, tiled=True)
    grad_features = (grad_snaked * (1.0 + jnp.sin(2.0 * snake_alpha * wide))).astype(jnp.bfloat16)
    grad_inner = grad_full[1:-1]
    scale = 1.0 / math.sqrt(blocks_out * lax.axis_size("tm"))
    lower = jnp.einsum(
        "ujr,up->pjr", local_tiled[:-1], grad_inner, preferred_element_type=jnp.float32
    )
    upper = jnp.einsum(
        "ujr,up->pjr", local_tiled[1:], grad_inner, preferred_element_type=jnp.float32
    )
    summed = lax.psum_scatter(
        jnp.concatenate([lower, upper], axis=1), "tm", scatter_dimension=0, tiled=True
    )
    grad_down = (summed * scale).astype(jnp.bfloat16)
    return (encoded, grad_features, grad_down)


def solution(mesh):
    placed = (P("tm", "chan"), P("chan"), P(None, None, "chan"), P("tm", "chan"))
    return jax.shard_map(
        shards,
        mesh=mesh,
        in_specs=placed,
        out_specs=(P("tm", "chan"), P("tm", "chan"), P("tm", None, "chan")),
        check_vma=False,
    )
```

profile of v0, /device:TPU:8, one launch (start us, length us, event | category | flops | bytes accessed | tf_op | source)
XLA Modules:
  0.0 450.1 jit_solution(14186953188106699410)
XLA Ops:
  7.2 0.0 reduce-scatter.3.cloned.1.call-start
  7.2 0.7 fusion.51
  7.9 1.7 collective-permute-start.3
  9.7 0.0 copy-start.4
  9.7 1.4 collective-permute-start.2
  11.1 2.5 fusion.49
  13.6 0.0 copy-start
  13.6 0.0 copy-start.2
  13.6 0.0 collective-permute-done.3
  13.6 0.0 copy-done.4
  13.6 1.9 fusion.12
  15.5 0.0 copy-done
  15.5 0.0 collective-permute-done.2
  15.5 0.1 copy-done.2
  15.6 6.7 %add_bitcast_fusion = f32[769,8,512]{2,0,1:T(8,128)} fusion(f32[769,512,8]{1,0,2:T(8,128)S(1)} %fusion.12, bf16[512,8,256]{2,1,0:T(8,128)(2,1)S(1)} %get-tuple-element.11, bf16[1,256]{1,0:T(2,128)(2,1)S(1)} %collective-permute-done.2, bf16[768,256]{1,0:T(8,128)(2,1)S(1)} %copy-done.4), kind=kOutput, calls=%fused_computation | convolution fusion | flops 1616647168 | bytes 27689472 | tf_op jit(solution)/shard_map/up,rjp->ujr/dot_general | solution.py:48
  22.3 16.4 %copy.59 = f32[769,8,512]{2,1,0:T(8,128)} copy(f32[769,8,512]{2,0,1:T(8,128)} %add_bitcast_fusion) | data formatting | bytes 25198592 | tf_op jit(solution)/shard_map/add | solution.py:48
  38.8 10.9 %slice.76 = f32[6144,512]{1,0:T(8,128)} slice(f32[6152,512]{1,0:T(8,128)} %bitcast.31), slice={[4:6148], [0:512]} | slice | bytes 25165824 | tf_op jit(solution)/shard_map/slice | solution.py:53
  49.6 0.0 copy-start.6
  49.6 0.0 reduce-scatter.3.cloned.1.call-update
  49.7 0.0 copy-start.5
  49.7 0.0 all-gather.5.cloned.1.call-start
  49.7 0.2 copy.19
  49.9 0.1 copy.18
  50.0 0.1 copy.20
  50.2 1.0 pad_maximum_fusion.3
  51.2 0.0 all-gather.5.cloned.1.call-update
  51.2 0.0 all-gather.3.cloned.1.call-start
  51.3 0.0 copy-done.6
  51.3 121.0 %reduce-scatter.3.cloned.1.call-done = f32[6144,128]{1,0:T(8,128)} async-done(((f32[6144,512]{1,0:T(8,128)}), f32[6144,128]{1,0:T(8,128)}) %reduce-scatter.3.cloned.1.call-update) | async-done | bytes 3145744 | tf_op jit(solution)/shard_map/reduce_scatter | solution.py:54
  172.3 0.0 copy-done.5
  172.3 23.1 %fusion.11 = (bf16[6144,128]{1,0:T(8,128)(2,1)}, bf16[6144,128]{1,0:T(8,128)(2,1)S(1)}) fusion(f32[6144,128]{1,0:T(8,128)} %reduce-scatter.3.cloned.1.call-done, bf16[6144,128]{1,0:T(8,128)(2,1)S(1)} %copy-done.5, f32[128]{0:T(128)S(1)} %broadcast_multiply_fusion, f32[128]{0:T(128)S(1)} %copy-done.6), kind=kLoop, calls=%fused_computation.19 | loop fusion | flops 7864320 | bytes 7865344 | tf_op jit(solution)/shard_map/convert_element_type | solution.py:55
  195.3 1.8 collective-permute-start
  197.1 1.3 collective-permute-start.1
  198.4 0.0 collective-permute-done
  198.4 3.0 collective-permute-done.1
  201.4 8.7 %concatenate.21 = bf16[6152,128]{1,0:T(8,128)(2,1)} concatenate(bf16[4,128]{1,0:T(4,128)(2,1)S(1)} %collective-permute-done, bf16[6144,128]{1,0:T(8,128)(2,1)S(1)} %get-tuple-element.16, bf16[4,128]{1,0:T(4,128)(2,1)S(1)} %collective-permute-done.1), dimensions={0} | concatenate | bytes 3149824 | tf_op jit(solution)/shard_map/concatenate | solution.py:19
  210.1 0.0 all-gather.3.cloned.1.call-update
  210.1 0.0 reduce-scatter.5.cloned.1.call-start
  210.2 1.6 fusion.18
  211.8 0.0 all-gather.5.cloned.1.call-done
  211.8 0.0 copy-start.7
  211.8 3.9 fusion.21
  215.7 0.0 copy-done.7
  215.7 1.8 fusion.19
  217.6 3.8 pad_maximum_fusion
  221.4 0.0 reduce-scatter.5.cloned.1.call-update
  221.4 0.0 copy-start.1
  221.4 63.4 %all-gather.3.cloned.1.call-done = bf16[6152,512]{1,0:T(8,128)(2,1)} async-done(((bf16[6152,128]{1,0:T(8,128)(2,1)}), bf16[6152,512]{1,0:T(8,128)(2,1)}) %all-gather.3.cloned.1.call-update) | async-done | bytes 6299664 | tf_op jit(solution)/shard_map/all_gather | solution.py:36
  284.8 5.3 %slice_bitcast_fusion.1 = (bf16[768,8,512]{2,1,0:T(8,128)(2,1)S(1)}, bf16[768,8,512]{2,1,0:T(8,128)(2,1)S(1)}) fusion(bf16[6152,512]{1,0:T(8,128)(2,1)} %all-gather.3.cloned.1.call-done), kind=kLoop, calls=%fused_computation.4 | loop fusion | bytes 25165824 | tf_op jit(solution)/shard_map/slice | solution.py:40
  290.1 0.0 copy-done.1
  290.1 0.0 copy-start.3
  290.1 3.9 fusion.28
  294.1 0.0 copy-done.3
  294.1 4.7 %fusion.38 = bf16[768,256]{1,0:T(8,128)(2,1)} fusion(f32[768,256]{1,0:T(8,128)S(1)} %fusion.28, bf16[512,8,256]{2,1,0:T(8,128)(2,1)S(1)} %copy-done.3, bf16[768,8,512]{2,1,0:T(8,128)(2,1)S(1)} %get-tuple-element.9), kind=kOutput, calls=%fused_computation.37 | convolution fusion | flops 1611005952 | bytes 9568256 | tf_op jit(solution)/shard_map/ujr,rjp->up/dot_general | solution.py:39
  298.8 143.3 %reduce-scatter.5.cloned.1.call-done = f32[16,16,128]{2,0,1:T(8,128)} async-done(((f32[1024,16,128]{2,0,1:T(8,128)}), f32[16,16,128]{2,0,1:T(8,128)}) %reduce-scatter.5.cloned.1.call-update) | async-done | bytes 131088 | tf_op jit(solution)/shard_map/reduce_scatter | solution.py:64
  442.0 0.9 multiply_convert_fusion
  443.0 0.6 copy.23
  (2 shorter events, 0.0 us)
Async XLA Ops:
  7.2 165.1 %reduce-scatter.3.cloned.1.call-start = ((), (), s32[]{:S(2)}) async-start(), calls=%async_computation.3 | async-start | bytes 15728640 | tf_op jit(solution)/shard_map/reduce_scatter | solution.py:54
  7.9 5.7 %collective-permute-start.3 = (bf16[1,256]{1,0:T(2,128)(2,1)S(1)}, bf16[1,256]{1,0:T(2,128)(2,1)S(1)}, u32[]{:S(2)}, u32[]{:S(2)}) collective-permute-start(bf16[1,256]{1,0:T(2,128)(2,1)S(1)} %get-tuple-element.20), channel_id=1, source_target_pairs={{0,4},{4,8},{8,12},{12,16},{16,20},{20,24},{24,28},{28,32},{32,36}... | collective-permute-start | bytes 1544 | tf_op jit(solution)/shard_map/ppermute | solution.py:15
  9.7 4.0 copy-start.4
  9.7 5.9 %collective-permute-start.2 = (bf16[1,256]{1,0:T(2,128)(2,1)S(1)}, bf16[1,256]{1,0:T(2,128)(2,1)S(1)}, u32[]{:S(2)}, u32[]{:S(2)}) collective-permute-start(bf16[1,256]{1,0:T(2,128)(2,1)S(1)} %get-tuple-element.19), channel_id=1, source_target_pairs={{4,0},{8,4},{12,8},{16,12},{20,16},{24,20},{28,24},{32,28},{36,32}... | collective-permute-start | bytes 1544 | tf_op jit(solution)/shard_map/ppermute | solution.py:18
  13.6 1.9 copy-start
  13.6 2.0 copy-start.2
  49.6 1.6 copy-start.6
  49.7 122.6 %copy-start.5 = (bf16[6144,128]{1,0:T(8,128)(2,1)S(1)}, bf16[6144,128]{1,0:T(8,128)(2,1)}, u32[]{:S(2)}) copy-start(bf16[6144,128]{1,0:T(8,128)(2,1)} %param.4) | copy-start | bytes 4718596
  49.7 162.1 %all-gather.5.cloned.1.call-start = ((), (), s32[]{:S(2)}) async-start(), calls=%async_computation.4 | async-start | bytes 2293760 | tf_op jit(solution)/shard_map/all_gather | solution.py:47
  51.2 233.6 %all-gather.3.cloned.1.call-start = ((), (), s32[]{:S(2)}) async-start(), calls=%async_computation.2 | async-start | bytes 7874560 | tf_op jit(solution)/shard_map/all_gather | solution.py:36
  195.3 3.1 collective-permute-start
  197.1 4.3 collective-permute-start.1
  210.1 231.9 %reduce-scatter.5.cloned.1.call-start = ((), (), s32[]{:S(2)}) async-start(), calls=%async_computation.5 | async-start | bytes 8519680 | tf_op jit(solution)/shard_map/reduce_scatter | solution.py:64
  211.8 3.9 copy-start.7
  221.4 68.7 %copy-start.1 = (bf16[512,8,256]{2,1,0:T(8,128)(2,1)S(1)}, bf16[512,8,256]{2,1,0:T(8,128)(2,1)}, u32[]{:S(2)}) copy-start(bf16[512,8,256]{2,1,0:T(8,128)(2,1)} %copy-done) | copy-start | bytes 6291460
  290.1 3.9 copy-start.3
Sparse Core Ops, SparseCore 0:
  49.8 122.4 reduce-scatter.2
  174.1 31.2 all-gather.4
  210.3 74.5 all-gather.2
  288.9 153.1 reduce-scatter.4
where the time goes:
time: 451 us; the launch traced here: 450 us
  waiting for transfers between devices  331 us (73%)
  local copies, waits for them, and re-layouts  45.7 us (10%)
  other arithmetic  30.4 us (7%)
  matrix products  23 us (5%)
  between operations  14 us (3%)
  starting transfers between devices  6.38 us (1%)
    reduce_scatter x1, waiting for transfers between devices, shards(): lax.psum_scatter(jnp.concatenate([lower, upper], axis=1), 'tm', scatter_d...  143 us
    reduce_scatter x1, waiting for transfers between devices, shards(): lax.psum_scatter(partial_terms, 'chan', scatter_dimension=1, tiled=True)  121 us
    all_gather x1, waiting for transfers between devices, shards(): full_cols = lax.all_gather(padded, 'chan', axis=1, tiled=True)  63.4 us
    convert_element_type x1, other arithmetic, shards(): (grad_snaked * (1.0 + jnp.sin(2.0 * snake_alpha * wide))).astype(jnp.bflo...  23.1 us
    add x1, local copies, waits for them, and re-layouts, shards(): jnp.einsum('up,rjp->ujr', grad_pad[1:], down_weight[:, :STRIDE], preferre...  16.4 us
    slice x1, local copies, waits for them, and re-layouts, shards(): spread.reshape(frames + STRIDE, down_weight.shape[0])  10.9 us
  transfers between devices with their start and end apart: 8, of which 4 were waited for; matrix products, arithmetic and copies ran while one was open for 14% of the time, Pallas kernels for 0%

commit v1 on v0

--- a/solution.py
+++ b/solution.py
@@ -5,6 +5,17 @@
 from jax.sharding import PartitionSpec as P
 
 STRIDE = 8
+
+
+def turned_line(x, name, d):
+    size = lax.axis_size(name)
+    route = [(i, (i + 1) % size) for i in range(size)]
+    parts = [x]
+    for far in range(1, size):
+        parts = [lax.ppermute(parts[0], name, route), *parts]
+    whole = jnp.concatenate(parts, axis=d)
+    shift = (lax.axis_index(name) + 1) * parts[-1].shape[d]
+    return jnp.roll(whole, shift, axis=d)
 
 
 def with_halo(block, sides, width):
@@ -33,7 +44,7 @@
     snaked = snake(wide, snake_alpha).astype(jnp.bfloat16)
     padded = with_halo(snaked, (("tm", 0),), offset)
     local_tiled = padded.reshape(blocks_out + 1, STRIDE, local_chans)
-    full_cols = lax.all_gather(padded, "chan", axis=1, tiled=True)
+    full_cols = turned_line(padded, "chan", 1)
     tiled = full_cols.reshape(blocks_out + 1, STRIDE, full_cols.shape[1])
     encoded = (
         jnp.einsum(

time: 451 us -> 379 us (0.84)
  waiting for transfers between devices: 331 us -> 235 us
  local copies, waits for them, and re-layouts: 45.7 us -> 61.6 us
  starting transfers between devices: 6.38 us -> 11.4 us
    reduce_scatter x1, waiting for transfers between devices: 143 us -> 17.5 us  [shards(): lax.psum_scatter(jnp.concatenate([lower, upper], axis=1), 'tm', scatter_d...]
    ppermute x0 -> x3, waiting for transfers between devices: none -> 98.1 us  [turned_line(): parts = [lax.ppermute(parts[0], name, route), *parts]]
    all_gather x1 -> x0, waiting for transfers between devices: 63.4 us -> none  [shards(): full_cols = lax.all_gather(padded, 'chan', axis=1, tiled=True)]
    unnamed x18 -> x27, local copies, waits for them, and re-layouts: 0.92 us -> 16.4 us
    concatenate x1, local copies, waits for them, and re-layouts: 8.69 us -> 2.58 us  [with_halo(): block = jnp.concatenate([low, block, high], axis=dim)]
    slice x1, local copies, waits for them, and re-layouts: 5.28 us -> 10.4 us  [shards(): tiled[:-1]]
  transfers between devices with their start and end apart: 8 -> 10, of which waited for: 4 -> 6; matrix products, arithmetic and copies ran while one was open for 14% -> 22% of each run, Pallas kernels for 0% -> 0%
where the time goes in v1:
time: 379 us
  waiting for transfers between devices  235 us (62%)
  local copies, waits for them, and re-layouts  61.6 us (16%)
  other arithmetic  30.9 us (8%)
  matrix products  26 us (7%)
  between operations  13.9 us (4%)
  starting transfers between devices  11.4 us (3%)
    reduce_scatter x1, waiting for transfers between devices, shards(): lax.psum_scatter(partial_terms, 'chan', scatter_dimension=1, tiled=True)  119 us
    ppermute x3, waiting for transfers between devices, turned_line(): parts = [lax.ppermute(parts[0], name, route), *parts]  98.1 us
    convert_element_type x1, other arithmetic, shards(): (grad_snaked * (1.0 + jnp.sin(2.0 * snake_alpha * wide))).astype(jnp.bflo...  23.1 us
    reduce_scatter x1, waiting for transfers between devices, shards(): lax.psum_scatter(jnp.concatenate([lower, upper], axis=1), 'tm', scatter_d...  17.5 us
    unnamed x27, local copies, waits for them, and re-layouts  16.4 us
    add x1, local copies, waits for them, and re-layouts, shards(): jnp.einsum('up,rjp->ujr', grad_pad[1:], down_weight[:, :STRIDE], preferre...  16.4 us
    slice x1, local copies, waits for them, and re-layouts, shards(): spread.reshape(frames + STRIDE, down_weight.shape[0])  10.9 us
    slice x1, local copies, waits for them, and re-layouts, shards(): tiled[:-1]  10.4 us
  transfers between devices with their start and end apart: 10, of which 6 were waited for; matrix products, arithmetic and copies ran while one was open for 22% of the time, Pallas kernels for 0%

profile of v1, /device:TPU:8, one launch (start us, length us, event | category | flops | bytes accessed | tf_op | source)
XLA Modules:
  0.0 378.9 jit_solution(18252492216030596628)
XLA Ops:
  7.2 0.0 reduce-scatter.3.cloned.1.call-start
  7.2 0.7 fusion.51
  7.9 1.3 collective-permute-start.5
  9.2 0.0 copy-start.5
  9.2 3.2 collective-permute-start.6
  12.4 2.5 fusion.49
  14.9 0.0 copy-start
  14.9 0.0 copy-start.2
  14.9 0.0 collective-permute-done.6
  14.9 0.0 copy-done.5
  14.9 1.9 fusion.12
  16.8 0.0 copy-done
  16.8 0.0 collective-permute-done.5
  16.8 0.1 copy-done.2
  16.9 6.7 %add_bitcast_fusion = f32[769,8,512]{2,0,1:T(8,128)} fusion(f32[769,512,8]{1,0,2:T(8,128)S(1)} %fusion.12, bf16[512,8,256]{2,1,0:T(8,128)(2,1)S(1)} %get-tuple-element.11, bf16[1,256]{1,0:T(2,128)(2,1)S(1)} %collective-permute-done.5, bf16[768,256]{1,0:T(8,128)(2,1)S(1)} %copy-done.5), kind=kOutput, calls=%fused_computation | convolution fusion | flops 1616647168 | bytes 27689472 | tf_op jit(solution)/shard_map/up,rjp->ujr/dot_general | solution.py:59
  23.6 16.4 %copy.59 = f32[769,8,512]{2,1,0:T(8,128)} copy(f32[769,8,512]{2,0,1:T(8,128)} %add_bitcast_fusion) | data formatting | bytes 25198592 | tf_op jit(solution)/shard_map/add | solution.py:59
  40.1 10.9 %slice.74 = f32[6144,512]{1,0:T(8,128)} slice(f32[6152,512]{1,0:T(8,128)} %bitcast.31), slice={[4:6148], [0:512]} | slice | bytes 25165824 | tf_op jit(solution)/shard_map/slice | solution.py:64
  50.9 0.0 copy-start.7
  50.9 0.0 reduce-scatter.3.cloned.1.call-update
  51.0 0.0 all-gather.2.cloned.1.call-start
  51.0 0.2 copy.19
  51.2 0.1 copy.18
  51.3 0.1 copy.20
  51.5 1.0 pad_maximum_fusion.3
  52.5 0.0 all-gather.2.cloned.1.call-update
  52.5 0.0 reduce-scatter.5.cloned.1.call-start
  52.6 0.0 copy-done.7
  52.6 118.7 %reduce-scatter.3.cloned.1.call-done = f32[6144,128]{1,0:T(8,128)} async-done(((f32[6144,512]{1,0:T(8,128)}), f32[6144,128]{1,0:T(8,128)}) %reduce-scatter.3.cloned.1.call-update) | async-done | bytes 3145744 | tf_op jit(solution)/shard_map/reduce_scatter | solution.py:65
  171.3 23.1 %fusion.11 = (bf16[6144,128]{1,0:T(8,128)(2,1)}, bf16[6144,128]{1,0:T(8,128)(2,1)S(1)}) fusion(f32[6144,128]{1,0:T(8,128)} %reduce-scatter.3.cloned.1.call-done, bf16[6144,128]{1,0:T(8,128)(2,1)} %param.4, f32[128]{0:T(128)S(1)} %broadcast_multiply_fusion, f32[128]{0:T(128)S(1)} %copy-done.7), kind=kLoop, calls=%fused_computation.19 | loop fusion | flops 7864320 | bytes 7865344 | tf_op jit(solution)/shard_map/convert_element_type | solution.py:66
  194.4 1.3 collective-permute-start.1
  195.7 3.0 collective-permute-start
  198.8 0.0 collective-permute-done.1
  198.8 0.8 collective-permute-done
  199.6 2.6 concatenate.27
  202.2 1.2 collective-permute-start.2
  203.4 2.0 fusion.18
  205.5 4.0 %fusion.21 = f32[1024,8,128]{2,0,1:T(8,128)S(1)} fusion(bf16[768,8,128]{2,1,0:T(8,128)(2,1)} %get-tuple-element.13, bf16[770,1024]{0,1:T(8,128)(2,1)} %all-gather.2.cloned.1.call-done), kind=kOutput, calls=%fused_computation.32 | convolution fusion | flops 1610612736 | bytes 7340032 | tf_op jit(solution)/shard_map/ujr,up->pjr/dot_general | solution.py:69
  209.4 0.0 copy-done.6
  209.4 0.0 copy-done.8
  209.4 1.9 fusion.19
  211.3 3.8 pad_maximum_fusion
  215.1 0.0 reduce-scatter.5.cloned.1.call-update
  215.1 24.4 %collective-permute-done.2 = bf16[6152,128]{1,0:T(8,128)(2,1)} collective-permute-done((bf16[6152,128]{1,0:T(8,128)(2,1)S(1)}, bf16[6152,128]{1,0:T(8,128)(2,1)}, u32[]{:S(2)}, u32[]{:S(2)}) %collective-permute-start.2) | collective-permute-done | bytes 1574944 | tf_op jit(solution)/shard_map/ppermute | solution.py:15
  239.5 1.2 collective-permute-start.3
  240.7 36.8 %collective-permute-done.3 = bf16[6152,128]{1,0:T(8,128)(2,1)S(1)} collective-permute-done((bf16[6152,128]{1,0:T(8,128)(2,1)}, bf16[6152,128]{1,0:T(8,128)(2,1)S(1)}, u32[]{:S(2)}, u32[]{:S(2)}) %collective-permute-start.3) | collective-permute-done | bytes 1574944 | tf_op jit(solution)/shard_map/ppermute | solution.py:15
  277.5 0.0 collective-permute-start.4
  277.5 36.9 %collective-permute-done.4 = bf16[6152,128]{1,0:T(8,128)(2,1)} collective-permute-done((bf16[6152,128]{1,0:T(8,128)(2,1)S(1)}, bf16[6152,128]{1,0:T(8,128)(2,1)}, u32[]{:S(2)}, u32[]{:S(2)}) %collective-permute-start.4) | collective-permute-done | bytes 1574944 | tf_op jit(solution)/shard_map/ppermute | solution.py:15
  314.4 2.9 constant_dynamic-update-slice_fusion.7
  317.3 1.4 constant_dynamic-update-slice_fusion.6
  318.7 2.8 constant_dynamic-update-slice_fusion.5
  321.6 1.4 constant_dynamic-update-slice_fusion.4
  322.9 2.8 constant_dynamic-update-slice_fusion.3
  325.7 1.4 constant_dynamic-update-slice_fusion.2
  327.1 2.8 constant_dynamic-update-slice_fusion.1
  329.9 1.3 constant_dynamic-update-slice_fusion
  331.3 10.4 %dynamic-slice_bitcast_fusion.1 = (bf16[768,8,512]{2,1,0:T(8,128)(2,1)}, bf16[768,8,512]{2,1,0:T(8,128)(2,1)}) fusion(bf16[6152,1024]{1,0:T(8,128)(2,1)} %constant_dynamic-update-slice_fusion, s32[]{:T(128)S(6)} %select_n.14, s32[]{:T(128)S(6)} %add.44), kind=kLoop, calls=%fused_computation.4 | loop fusion | bytes 25165832 | tf_op jit(solution)/shard_map/slice | solution.py:51
  341.7 0.0 copy-done.1
  341.7 7.0 %fusion.28 = f32[768,256]{1,0:T(8,128)S(1)} fusion(bf16[512,8,256]{2,1,0:T(8,128)(2,1)S(1)} %copy-done.1, bf16[768,8,512]{2,1,0:T(8,128)(2,1)} %get-tuple-element.10), kind=kOutput, calls=%fused_computation.35 | convolution fusion | flops 1610612736 | bytes 9175040 | tf_op jit(solution)/shard_map/ujr,rjp->up/dot_general | solution.py:53
  348.7 0.0 copy-done.3
  348.7 0.0 copy-done.4
  348.7 4.7 %fusion.38 = bf16[768,256]{1,0:T(8,128)(2,1)} fusion(f32[768,256]{1,0:T(8,128)S(1)} %fusion.28, bf16[512,8,256]{2,1,0:T(8,128)(2,1)S(1)} %copy-done.3, bf16[768,8,512]{2,1,0:T(8,128)(2,1)S(1)} %copy-done.4), kind=kOutput, calls=%fused_computation.37 | convolution fusion | flops 1611005952 | bytes 9568256 | tf_op jit(solution)/shard_map/ujr,rjp->up/dot_general | solution.py:50
  353.4 17.5 %reduce-scatter.5.cloned.1.call-done = f32[16,16,128]{2,0,1:T(8,128)} async-done(((f32[1024,16,128]{2,0,1:T(8,128)}), f32[16,16,128]{2,0,1:T(8,128)}) %reduce-scatter.5.cloned.1.call-update) | async-done | bytes 131088 | tf_op jit(solution)/shard_map/reduce_scatter | solution.py:75
  370.8 0.9 multiply_convert_fusion
  371.8 0.6 copy.23
  (8 shorter events, 0.0 us)
Async XLA Ops:
  7.2 164.1 %reduce-scatter.3.cloned.1.call-start = ((), (), s32[]{:S(2)}) async-start(), calls=%async_computation.2 | async-start | bytes 15728640 | tf_op jit(solution)/shard_map/reduce_scatter | solution.py:65
  7.9 8.9 %collective-permute-start.5 = (bf16[1,256]{1,0:T(2,128)(2,1)S(1)}, bf16[1,256]{1,0:T(2,128)(2,1)S(1)}, u32[]{:S(2)}, u32[]{:S(2)}) collective-permute-start(bf16[1,256]{1,0:T(2,128)(2,1)S(1)} %get-tuple-element.19), channel_id=1, source_target_pairs={{4,0},{8,4},{12,8},{16,12},{20,16},{24,20},{28,24},{32,28},{36,32}... | collective-permute-start | bytes 1544 | tf_op jit(solution)/shard_map/ppermute | solution.py:29
  9.2 5.7 %copy-start.5 = (bf16[768,256]{1,0:T(8,128)(2,1)S(1)}, bf16[768,256]{1,0:T(8,128)(2,1)}, u32[]{:S(2)}) copy-start(bf16[768,256]{1,0:T(8,128)(2,1)} %param.7) | copy-start | bytes 1179652
  9.2 5.7 %collective-permute-start.6 = (bf16[1,256]{1,0:T(2,128)(2,1)S(1)}, bf16[1,256]{1,0:T(2,128)(2,1)S(1)}, u32[]{:S(2)}, u32[]{:S(2)}) collective-permute-start(bf16[1,256]{1,0:T(2,128)(2,1)S(1)} %get-tuple-element.20), channel_id=1, source_target_pairs={{0,4},{4,8},{8,12},{12,16},{16,20},{20,24},{24,28},{28,32},{32,36}... | collective-permute-start | bytes 1544 | tf_op jit(solution)/shard_map/ppermute | solution.py:26
  14.9 1.9 copy-start
  14.9 2.0 copy-start.2
  50.9 1.7 copy-start.7
  51.0 154.5 %all-gather.2.cloned.1.call-start = ((), (), s32[]{:S(2)}) async-start(), calls=%async_computation.3 | async-start | bytes 2293760 | tf_op jit(solution)/shard_map/all_gather | solution.py:58
  52.5 318.3 %reduce-scatter.5.cloned.1.call-start = ((), (), s32[]{:S(2)}) async-start(), calls=%async_computation.4 | async-start | bytes 8519680 | tf_op jit(solution)/shard_map/reduce_scatter | solution.py:75
  194.4 4.3 %collective-permute-start.1 = (bf16[4,128]{1,0:T(4,128)(2,1)S(1)}, bf16[4,128]{1,0:T(4,128)(2,1)S(1)}, u32[]{:S(2)}, u32[]{:S(2)}) collective-permute-start(bf16[4,128]{1,0:T(4,128)(2,1)S(1)} %get-tuple-element.17), channel_id=1, source_target_pairs={{4,0},{8,4},{12,8},{16,12},{20,16},{24,20},{28,24},{32,28},{36,32}... | collective-permute-start | bytes 3080 | tf_op jit(solution)/shard_map/ppermute | solution.py:29
  195.7 3.8 %collective-permute-start = (bf16[4,128]{1,0:T(4,128)(2,1)S(1)}, bf16[4,128]{1,0:T(4,128)(2,1)S(1)}, u32[]{:S(2)}, u32[]{:S(2)}) collective-permute-start(bf16[4,128]{1,0:T(4,128)(2,1)S(1)} %get-tuple-element.18), channel_id=1, source_target_pairs={{0,4},{4,8},{8,12},{12,16},{16,20},{20,24},{24,28},{28,32},{32,36}... | collective-permute-start | bytes 3080 | tf_op jit(solution)/shard_map/ppermute | solution.py:26
  202.2 37.3 %collective-permute-start.2 = (bf16[6152,128]{1,0:T(8,128)(2,1)S(1)}, bf16[6152,128]{1,0:T(8,128)(2,1)}, u32[]{:S(2)}, u32[]{:S(2)}) collective-permute-start(bf16[6152,128]{1,0:T(8,128)(2,1)S(1)} %concatenate.27), channel_id=1, source_target_pairs={{0,1},{1,2},{2,3},{3,0},{4,5},{5,6},{6,7},{7,4},{8,9},{9,10},{10,1... | collective-permute-start | bytes 4724744 | tf_op jit(solution)/shard_map/ppermute | solution.py:15
  205.5 4.0 %copy-start.6 = (bf16[768,8,128]{2,1,0:T(8,128)(2,1)S(1)}, bf16[768,8,128]{2,1,0:T(8,128)(2,1)}, u32[]{:S(2)}) copy-start(bf16[768,8,128]{2,1,0:T(8,128)(2,1)} %get-tuple-element.14) | copy-start | bytes 4718596
  205.5 4.0 %copy-start.8 = (bf16[770,1024]{0,1:T(8,128)(2,1)S(1)}, bf16[770,1024]{0,1:T(8,128)(2,1)}, u32[]{:S(2)}) copy-start(bf16[770,1024]{0,1:T(8,128)(2,1)} %all-gather.2.cloned.1.call-done) | copy-start | bytes 4730884
  239.5 38.0 %collective-permute-start.3 = (bf16[6152,128]{1,0:T(8,128)(2,1)}, bf16[6152,128]{1,0:T(8,128)(2,1)S(1)}, u32[]{:S(2)}, u32[]{:S(2)}) collective-permute-start(bf16[6152,128]{1,0:T(8,128)(2,1)} %collective-permute-done.2), channel_id=1, source_target_pairs={{0,1},{1,2},{2,3},{3,0},{4,5},{5,6},{6,7},{7,4},{8,9},{9,10},{10,1... | collective-permute-start | bytes 4724744 | tf_op jit(solution)/shard_map/ppermute | solution.py:15
  277.5 36.9 %collective-permute-start.4 = (bf16[6152,128]{1,0:T(8,128)(2,1)S(1)}, bf16[6152,128]{1,0:T(8,128)(2,1)}, u32[]{:S(2)}, u32[]{:S(2)}) collective-permute-start(bf16[6152,128]{1,0:T(8,128)(2,1)S(1)} %collective-permute-done.3), channel_id=1, source_target_pairs={{0,1},{1,2},{2,3},{3,0},{4,5},{5,6},{6,7},{7,4},{8,9},{9,10},{10,1... | collective-permute-start | bytes 4724744 | tf_op jit(solution)/shard_map/ppermute | solution.py:15
  331.3 10.4 %copy-start.1 = (bf16[512,8,256]{2,1,0:T(8,128)(2,1)S(1)}, bf16[512,8,256]{2,1,0:T(8,128)(2,1)}, u32[]{:S(2)}) copy-start(bf16[512,8,256]{2,1,0:T(8,128)(2,1)} %copy-done) | copy-start | bytes 6291460
  341.7 7.0 %copy-start.3 = (bf16[512,8,256]{2,1,0:T(8,128)(2,1)S(1)}, bf16[512,8,256]{2,1,0:T(8,128)(2,1)}, u32[]{:S(2)}) copy-start(bf16[512,8,256]{2,1,0:T(8,128)(2,1)} %copy-done.2) | copy-start | bytes 6291460
  341.7 7.0 %copy-start.4 = (bf16[768,8,512]{2,1,0:T(8,128)(2,1)S(1)}, bf16[768,8,512]{2,1,0:T(8,128)(2,1)}, u32[]{:S(2)}) copy-start(bf16[768,8,512]{2,1,0:T(8,128)(2,1)} %get-tuple-element.9) | copy-start | bytes 18874372
Sparse Core Ops, SparseCore 0:
  51.1 120.1 reduce-scatter.2
  173.1 31.2 all-gather.1
  215.2 155.5 reduce-scatter.4
